TPU v7x, 32 devices: a whole 2x2x4 slice. The times are simulated.
32 devices in a mesh: groups: 2 (over y), tensor: 16 (over z, x, core).
Axes of the slice: x: 2, y: 2, z: 4, core: 2. Of those that a mesh axis runs over, the one named last changes fastest.
Arguments:
- grad_out: bfloat16 [64, 8192], P(('groups', 'tensor')), parts along dimension 0, may hold values from -6 to 6
- hidden: bfloat16 [64, 28672], P('groups', 'tensor'), parts along dimension 0, may hold values from -1 to 1
- down_weight: bfloat16 [28672, 8192], P('tensor'), may hold values from -0.03125 to 0.03125
- proj_in: bfloat16 [28672, 64], P('tensor'), may hold values from -0.1875 to 0.1875
- proj_out: bfloat16 [8192, 64], replicated, may hold values from -0.0625 to 0.0625
- example_lengths: int32 [32], P('groups'), parts along dimension 0, may hold values from 1 to 8, 32 in all
- owner_counts: int32 [32], P('groups'), parts along dimension 0, may hold values from 0 to 3, as said below
Outputs:
- grad_weight: bfloat16 [57344, 8192], P(('groups', 'tensor')), parts along dimension 0
- grad_hidden: bfloat16 [64, 28672], P('groups', 'tensor'), parts along dimension 0
- sketches: float32 [96, 4096], P(('groups', 'tensor')), parts along dimension 0
There are 2 independent parts, one for each index of `groups`. A program takes and returns all parts, laid end to end along the dimension named above; an argument that names none is the same for every part. Nothing has to cross between parts.
Inputs may be any that keep to these rules, and one draw needn't show every extreme that they name: Example e covers the next example_lengths[e] tokens after the examples before it; the lengths sum to 32; some example has exactly 8 tokens. `owner_counts`: owner o owns the examples that begin at the sum of the counts of the owners before it, in order; the counts sum to 16; some owner holds exactly 3.
All inputs are finite; a program needn't handle non-finite values.
Results may differ from a plain program's by a relative error of at most 0.001.
Values may be sent and summed in bfloat16 or wider, within the bound.
A program may use at most 128 MiB of HBM per device.

v0:
```python
import jax
import jax.numpy as jnp
from jax import lax
from jax.sharding import PartitionSpec as P

OWN_CAP = 3


def table_lookup(table, index):
    hits = index[:, None] == jnp.arange(table.shape[0], dtype=jnp.int32)[None, :]
    return jnp.sum(jnp.where(hits, table[None, :], 0), axis=1)


def slot_bounds(example_lengths, owner_counts, slot_ids, slot_cap):
    example_start = jnp.cumsum(example_lengths) - example_lengths
    owner_first = jnp.cumsum(owner_counts) - owner_counts
    slot_owner = slot_ids // slot_cap
    slot_place = slot_ids % slot_cap
    slot_live = slot_place < table_lookup(owner_counts, slot_owner)
    example_id = table_lookup(owner_first, slot_owner) + slot_place
    begin_token = table_lookup(example_start, example_id)
    end_token = begin_token + table_lookup(example_lengths, example_id)
    return (begin_token, end_token, slot_live)


def layer_rows(hidden, down_weight, weight_total, grad_hidden, grad_piece):
    weight_total = lax.dot_general(
        hidden, grad_piece, (((0,), (0,)), ((), ())), preferred_element_type=jnp.float32
    )
    grad_block = lax.dot_general(
        grad_piece, down_weight, (((1,), (1,)), ((), ())), preferred_element_type=jnp.float32
    )
    grad_hidden = grad_block.astype(jnp.bfloat16)
    return (weight_total, grad_hidden)


def shards(grad_out, hidden, down_weight, proj_in, proj_out, example_lengths, owner_counts):
    token_total = hidden.shape[0]
    hidden_width = hidden.shape[1]
    model_width = grad_out.shape[1]
    rank_width = proj_out.shape[1]
    partial_proj = jnp.dot(hidden, proj_in, preferred_element_type=jnp.float32)
    summed_proj = lax.psum(partial_proj, "tensor")
    weight_init = jnp.zeros((hidden_width, model_width), jnp.float32)
    hidden_init = jnp.zeros((token_total, hidden_width), jnp.bfloat16)
    grad_piece = lax.all_gather(grad_out, "tensor", axis=0, tiled=True)
    weight_total, grad_hidden = layer_rows(
        hidden, down_weight, weight_init, hidden_init, grad_piece
    )
    projected = jnp.dot(grad_piece, proj_out, preferred_element_type=jnp.float32)
    weight_total, grad_hidden, grad_proj = (weight_total, grad_hidden, projected)
    own_ids = lax.axis_index("tensor") * OWN_CAP + jnp.arange(OWN_CAP, dtype=jnp.int32)
    begin_token, end_token, slot_live = slot_bounds(example_lengths, owner_counts, own_ids, OWN_CAP)
    positions = jnp.arange(token_total, dtype=jnp.int32)
    own_member = (
        (positions[None, :] >= begin_token[:, None])
        & (positions[None, :] < end_token[:, None])
        & slot_live[:, None]
    ).astype(jnp.float32)
    weighted = own_member[:, :, None] * summed_proj[None, :, :]
    sketches = jnp.einsum(
        "sti,tk->sik",
        weighted,
        grad_proj,
        precision=lax.Precision.HIGHEST,
        preferred_element_type=jnp.float32,
    )
    sketches = sketches.reshape(OWN_CAP, rank_width * rank_width)
    return (weight_total.astype(jnp.bfloat16), grad_hidden, sketches)


def solution(mesh):
    return jax.shard_map(
        shards,
        mesh=mesh,
        in_specs=(
            P(("groups", "tensor"), None),
            P("groups", "tensor"),
            P("tensor", None),
            P("tensor", None),
            P(),
            P("groups"),
            P("groups"),
        ),
        out_specs=(
            P(("groups", "tensor"), None),
            P("groups", "tensor"),
            P(("groups", "tensor"), None),
        ),
        check_vma=False,
    )
```

profile of v0, /device:TPU:0, one launch (start us, length us, event | category | flops | bytes accessed | tf_op | source)
XLA Modules:
  0.0 116.4 jit_solution(11824403140868927190)
XLA Ops:
  0.6 0.0 copy-start
  0.6 24.9 %all-gather = bf16[16,2,8192]{2,1,0:T(2,128)(2,1)S(1)} all-gather(bf16[1,2,8192]{2,1,0:T(2,128)(2,1)} %bitcast.14), channel_id=1, replica_groups=mesh['groups'=2,'tensor'=16] {'tensor'}, dimensions={0}, use_global_device_ids=true | all-gather | bytes 557056 | tf_op jit(solution)/shard_map/all_gather | solution.py:46
  25.6 0.2 reshape.161
  25.8 15.2 %convolution_convert_fusion = bf16[1792,8192]{1,0:T(8,128)(2,1)} fusion(bf16[32,1792]{1,0:T(8,128)(2,1)} %param.8, bf16[32,8192]{1,0:T(8,128)(2,1)S(1)} %reshape.161), kind=kOutput, calls=%fused_computation | convolution fusion | flops 954204160 | bytes 29999104 | tf_op jit(solution)/shard_map/dot_general | solution.py:27
  41.0 0.0 copy-start.1
  41.0 0.0 copy-start.2
  41.0 0.0 copy-start.3
  41.0 0.0 copy-start.4
  41.0 14.8 %convolution_convert_fusion.1 = bf16[32,1792]{1,0:T(8,128)(2,1)} fusion(bf16[32,8192]{1,0:T(8,128)(2,1)S(1)} %reshape.161, bf16[1792,8192]{1,0:T(8,128)(2,1)} %param.9), kind=kOutput, calls=%fused_computation.1 | convolution fusion | flops 939581440 | bytes 29999104 | tf_op jit(solution)/shard_map/dot_general | solution.py:30
  55.8 0.0 copy-done
  55.8 0.4 convolution_bitcast_fusion
  56.2 0.0 copy-done.1
  56.2 0.0 copy-done.2
  56.2 0.2 fusion.10
  56.4 57.9 %psum.7 = f32[32,64]{1,0:T(8,128)S(1)} all-reduce(f32[32,64]{1,0:T(8,128)S(1)} %fusion.10), channel_id=1, replica_groups=mesh['groups'=2,'tensor'=16] {'tensor'}, use_global_device_ids=true, to_apply=%region_6.7 | all-reduce | flops 2048 | bytes 16384 | tf_op jit(solution)/shard_map/psum | solution.py:43
  114.2 0.0 copy-done.3
  114.3 0.1 copy.16
  114.4 0.1 reduce
  114.5 0.2 select_reduce_fusion
  114.7 0.0 copy-done.4
  114.7 0.1 copy.17
  114.8 0.1 reduce.1
  115.0 0.2 select_reduce_fusion.1
  115.2 0.1 fusion.6
  115.2 0.4 fusion
  115.7 0.7 reshape.159
  (8 shorter events, 0.1 us)
Async XLA Ops:
  0.6 55.2 %copy-start = (bf16[8192,64]{0,1:T(8,128)(2,1)S(1)}, bf16[8192,64]{0,1:T(8,128)(2,1)}, u32[]{:S(2)}) copy-start(bf16[8192,64]{0,1:T(8,128)(2,1)} %param.11) | copy-start | bytes 3145732
  41.0 15.2 %copy-start.1 = (bf16[32,1792]{1,0:T(8,128)(2,1)S(1)}, bf16[32,1792]{1,0:T(8,128)(2,1)}, u32[]{:S(2)}) copy-start(bf16[32,1792]{1,0:T(8,128)(2,1)} %param.8) | copy-start | bytes 344068
  41.0 15.2 %copy-start.2 = (bf16[1792,64]{0,1:T(8,128)(2,1)S(1)}, bf16[1792,64]{0,1:T(8,128)(2,1)}, u32[]{:S(2)}) copy-start(bf16[1792,64]{0,1:T(8,128)(2,1)} %param.10) | copy-start | bytes 688132
  41.0 73.2 %copy-start.3 = (s32[16]{0:T(128)S(1)}, s32[16]{0:T(128)}, u32[]{:S(2)}) copy-start(s32[16]{0:T(128)} %param.13) | copy-start | bytes 196
  41.0 73.7 %copy-start.4 = (s32[16]{0:T(128)S(1)}, s32[16]{0:T(128)}, u32[]{:S(2)}) copy-start(s32[16]{0:T(128)} %param.12) | copy-start | bytes 196
where the time goes:
time: 117 us; the launch traced here: 116 us
  blocking collectives  82.8 us (71%)
  matrix products  31 us (26%)
    psum x1, blocking collectives, shards(): summed_proj = lax.psum(partial_proj, 'tensor')  57.9 us
    all_gather x1, blocking collectives, shards(): grad_piece = lax.all_gather(grad_out, 'tensor', axis=0, tiled=True)  24.9 us
    dot_general x1, matrix products, layer_rows(): lax.dot_general(hidden, grad_piece, (((0,), (0,)), ((), ())), preferred_e...  15.2 us
    dot_general x1, matrix products, layer_rows(): lax.dot_general(grad_piece, down_weight, (((1,), (1,)), ((), ())), prefer...  14.8 us

commit v1 on v0

v1 whole, which is shorter than its diff:
```python
import functools
import jax
import jax.numpy as jnp
from jax import lax
from jax.experimental import pallas as pl
from jax.experimental.pallas import tpu as pltpu
from jax.sharding import PartitionSpec as P

OWN_CAP = 3
SLOW = 4
NT = (((1,), (1,)), ((), ()))
TN = (((0,), (0,)), ((), ()))
F32 = jnp.float32
BF16 = jnp.bfloat16


def row_tile(width):
    return 256 if width % 256 == 0 else width


def gather_kernel(
    fast, g_ref, hid_ref, pin_ref, w_ref, all_ref, gh_ref, hp_ref,
    buf, wide, wbuf, part, stage_a, stage_b, stage_c, wsem,
    s1s, s1r, s2s, s2r, s3s, s3r, pas, par, pbs, pbr, pcs, pcr,
):
    me = lax.axis_index("tensor")
    core = lax.rem(me, 2)
    chip = lax.div(me, 2)
    b = lax.rem(chip, fast)
    a = lax.div(chip, fast)
    blocks = buf.shape[0]
    rows = wbuf.shape[0]
    tile = row_tile(rows)
    tiles = rows // tile

    for i in range(tiles):
        pltpu.make_async_copy(
            w_ref.at[pl.ds(i * tile, tile)], wbuf.at[pl.ds(i * tile, tile)], wsem.at[i]
        ).start()

    def index(ai, bi, ci):
        return (ai * fast + bi) * 2 + ci

    def up(value, step, size):
        return lax.rem(value + step, size)

    def down(value, step, size):
        return lax.rem(value + size - step, size)

    barrier = pltpu.get_barrier_semaphore()
    peers = [index(up(a, s, SLOW), b, core) for s in range(1, SLOW)]
    peers += [index(a, up(b, r, fast), core) for r in range(1, fast)]
    peers += [index(a, b, 1 - core)]
    for peer in peers:
        pl.semaphore_signal(barrier, inc=1, device_id={"tensor": peer}, device_id_type=pl.DeviceIdType.MESH)
    buf[me] = g_ref[...]
    part[0] = lax.dot_general(hid_ref[...], pin_ref[...], NT, preferred_element_type=F32)
    pl.semaphore_wait(barrier, len(peers))

    def send(src, dst, ssem, rsem, peer):
        return pltpu.make_async_remote_copy(
            src_ref=src, dst_ref=dst, send_sem=ssem, recv_sem=rsem,
            device_id={"tensor": peer}, device_id_type=pl.DeviceIdType.MESH,
        )

    sends = []

    def go(copy):
        copy.start()
        sends.append(copy)

    def block(i):
        return buf.at[i]

    def to_sibling(s, r):
        i = index(down(a, s, SLOW), down(b, r, fast), core)
        go(send(block(i), block(i), s3s.at[s, r], s3r.at[s, r], index(a, b, 1 - core)))

    def to_fast(s):
        i = index(down(a, s, SLOW), b, core)
        for r in range(1, fast):
            go(send(block(i), block(i), s2s.at[s, r], s2r.at[s, r], index(a, up(b, r, fast), core)))
        to_sibling(s, 0)

    def landed(s, r, c, sem):
        i = index(down(a, s, SLOW), down(b, r, fast), c)
        send(block(i), block(i), sem, sem, index(a, b, 1 - core)).wait_recv()

    for s in (2, 1, 3):
        go(send(block(me), block(me), s1s.at[s], s1r.at[s], index(up(a, s, SLOW), b, core)))
    to_fast(0)
    for s in range(1, SLOW):
        go(send(part.at[0], stage_a.at[s], pas.at[s], par.at[s], index(up(a, s, SLOW), b, core)))
    for s in (1, 3, 2):
        landed(s, 0, core, s1r.at[s])
        to_fast(s)
    total = part[0]
    for s in range(1, SLOW):
        send(stage_a.at[s], stage_a.at[s], par.at[s], par.at[s], index(a, b, 1 - core)).wait_recv()
        total = total + stage_a[s]
    part[1] = total
    for r in range(1, fast):
        go(send(part.at[1], stage_b.at[r], pbs.at[r], pbr.at[r], index(a, up(b, r, fast), core)))
    for s in (0, 1, 3, 2):
        for r in range(1, fast):
            landed(s, r, core, s2r.at[s, r])
            to_sibling(s, r)
    for r in range(1, fast):
        send(stage_b.at[r], stage_b.at[r], pbr.at[r], pbr.at[r], index(a, b, 1 - core)).wait_recv()
        total = total + stage_b[r]
    part[2] = total
    go(send(part.at[2], stage_c.at[0], pcs.at[0], pcr.at[0], index(a, b, 1 - core)))
    for s in (0, 1, 3, 2):
        for r in range(fast):
            landed(s, r, 1 - core, s3r.at[s, r])

    width = buf.shape[2]
    per = buf.shape[1]
    for d in range(blocks):
        wide[d * per : (d + 1) * per, :] = buf[d].astype(F32)
    all_ref[...] = wide[...].astype(BF16)

    for i in range(tiles):
        pltpu.make_async_copy(
            w_ref.at[pl.ds(i * tile, tile)], wbuf.at[pl.ds(i * tile, tile)], wsem.at[i]
        ).wait()
        gh_ref[:, i * tile : (i + 1) * tile] = lax.dot_general(
            all_ref[...], wbuf[i * tile : (i + 1) * tile, :], NT, preferred_element_type=F32
        ).astype(BF16)

    send(stage_c.at[0], stage_c.at[0], pcr.at[0], pcr.at[0], index(a, b, 1 - core)).wait_recv()
    hp_ref[...] = total + stage_c[0]
    for copy in sends:
        copy.wait_send()


def gather(tensor, g, hidden, pin_t, w):
    per, width = g.shape
    tokens, rows = hidden.shape
    rank = pin_t.shape[0]
    fast = tensor // (2 * SLOW)
    dma = pltpu.SemaphoreType.DMA
    vmem = pl.BlockSpec(memory_space=pltpu.VMEM)
    return pl.pallas_call(
        functools.partial(gather_kernel, fast),
        out_shape=(
            jax.ShapeDtypeStruct((tokens, width), BF16),
            jax.ShapeDtypeStruct((tokens, rows), BF16),
            jax.ShapeDtypeStruct((tokens, rank), F32),
        ),
        in_specs=[vmem, vmem, vmem, pl.BlockSpec(memory_space=pl.ANY)],
        out_specs=(vmem, vmem, vmem),
        scratch_shapes=[
            pltpu.VMEM((tensor, per, width), BF16),
            pltpu.VMEM((tokens, width), F32),
            pltpu.VMEM((rows, width), BF16),
            pltpu.VMEM((3, tokens, rank), F32),
            pltpu.VMEM((SLOW, tokens, rank), F32),
            pltpu.VMEM((fast, tokens, rank), F32),
            pltpu.VMEM((1, tokens, rank), F32),
            dma((rows // row_tile(rows),)),
            dma((SLOW,)), dma((SLOW,)),
            dma((SLOW, fast)), dma((SLOW, fast)),
            dma((SLOW, fast)), dma((SLOW, fast)),
            dma((SLOW,)), dma((SLOW,)),
            dma((fast,)), dma((fast,)),
            dma((1,)), dma((1,)),
        ],
        compiler_params=pltpu.CompilerParams(
            collective_id=0, has_side_effects=True, vmem_limit_bytes=58 * 2**20
        ),
        name="gather_and_grad_hidden",
    )(g, hidden, pin_t, w)


def weight_kernel(
    len_ref, cnt_ref, me_ref, hid_ref, all_ref, gh_in, hp_ref, pout_ref,
    gw_ref, gh_ref, sk_ref,
):
    gw_ref[...] = lax.dot_general(
        hid_ref[...], all_ref[...], TN, preferred_element_type=F32
    ).astype(BF16)

    @pl.when(pl.program_id(0) == 1 % pl.num_programs(0))
    def _():
        gh_ref[...] = gh_in[...]
        tokens, rank = hp_ref.shape
        me = me_ref[0]
        owners = cnt_ref.shape[0]
        examples = len_ref.shape[0]
        first = lax.fori_loop(0, owners, lambda k, c: c + jnp.where(k < me, cnt_ref[k], 0), jnp.int32(0))
        mine = cnt_ref[me]
        gp = lax.dot_general(all_ref[...], pout_ref[...], NT, preferred_element_type=F32)
        gp = jnp.concatenate([gp, gp], axis=1)
        t = lax.broadcasted_iota(jnp.int32, (tokens, rank), 0)
        left = lax.broadcasted_iota(jnp.int32, (1, 2 * rank), 1) < rank
        for j in range(OWN_CAP):
            e = first + j
            begin, end = lax.fori_loop(
                0, examples,
                lambda k, c: (c[0] + jnp.where(k < e, len_ref[k], 0), c[1] + jnp.where(k <= e, len_ref[k], 0)),
                (jnp.int32(0), jnp.int32(0)),
            )
            end = jnp.where(j < mine, end, begin)
            hp = jnp.where((t >= begin) & (t < end), hp_ref[...], 0.0)
            s = lax.dot_general(
                hp, gp, TN, precision=lax.Precision.HIGHEST, preferred_element_type=F32
            )
            for p in range(rank // 2):
                sk_ref[j : j + 1, 2 * p * rank : 2 * (p + 1) * rank] = jnp.where(
                    left, s[2 * p : 2 * p + 1, :], s[2 * p + 1 : 2 * p + 2, :]
                )


def weight(hidden, everyone, gh, hp, pout_t, lengths, counts, me):
    tokens, rows = hidden.shape
    width = everyone.shape[1]
    rank = hp.shape[1]
    tile = 128 if rows % 128 == 0 else rows
    whole = lambda i: (0, 0)
    smem = pl.BlockSpec(memory_space=pltpu.SMEM)
    return pl.pallas_call(
        weight_kernel,
        grid=(rows // tile,),
        in_specs=[
            smem, smem, smem,
            pl.BlockSpec((tokens, tile), lambda i: (0, i)),
            pl.BlockSpec((tokens, width), whole),
            pl.BlockSpec((tokens, rows), whole),
            pl.BlockSpec((tokens, rank), whole),
            pl.BlockSpec((rank, width), whole),
        ],
        out_specs=(
            pl.BlockSpec((tile, width), lambda i: (i, 0)),
            pl.BlockSpec((tokens, rows), whole),
            pl.BlockSpec((OWN_CAP, rank * rank), whole),
        ),
        out_shape=(
            jax.ShapeDtypeStruct((rows, width), BF16),
            jax.ShapeDtypeStruct((tokens, rows), BF16),
            jax.ShapeDtypeStruct((OWN_CAP, rank * rank), F32),
        ),
        compiler_params=pltpu.CompilerParams(vmem_limit_bytes=58 * 2**20),
        name="grad_weight_and_sketches",
    )(lengths, counts, me, hidden, everyone, gh, hp, pout_t)


def solution(mesh):
    tensor = mesh.shape["tensor"]

    def shards(grad_out, hidden, down_weight, proj_in, proj_out, example_lengths, owner_counts):
        everyone, gh, hp = gather(tensor, grad_out, hidden, proj_in.T, down_weight)
        me = lax.axis_index("tensor").astype(jnp.int32).reshape(1)
        return weight(hidden, everyone, gh, hp, proj_out.T, example_lengths, owner_counts, me)

    return jax.shard_map(
        shards,
        mesh=mesh,
        in_specs=(
            P(("groups", "tensor"), None),
            P("groups", "tensor"),
            P("tensor", None),
            P("tensor", None),
            P(),
            P("groups"),
            P("groups"),
        ),
        out_specs=(
            P(("groups", "tensor"), None),
            P("groups", "tensor"),
            P(("groups", "tensor"), None),
        ),
        check_vma=False,
    )
```

time: 117 us -> 50.6 us (0.43)
  blocking collectives: 82.8 us -> 0 us
  Pallas kernels: 0 us -> 49.4 us
  matrix products: 31 us -> 0 us
    psum x1 -> x0, blocking collectives: 57.9 us -> none  [shards(): summed_proj = lax.psum(partial_proj, 'tensor')]
    pallas_call x0 -> x2, Pallas kernels: none -> 49.4 us  [the longest x1 31.1 us: gather(): pl.pallas_call(functools.partial(gather_kernel, fast), out_shape=(jax.Sha...]
    dot_general x5 -> x0, matrix products: 31 us -> none  [the longest x1 15.2 us: layer_rows(): lax.dot_general(hidden, grad_piece, (((0,), (0,)), ((), ())), preferred_e...]
    all_gather x1 -> x0, blocking collectives: 24.9 us -> none  [shards(): grad_piece = lax.all_gather(grad_out, 'tensor', axis=0, tiled=True)]
where the time goes in v1:
time: 50.6 us; the launch traced here: 50.1 us
  Pallas kernels  49.4 us (98%)
  between operations  0.64 us (1%)
    pallas_call x1, Pallas kernels, gather(): pl.pallas_call(functools.partial(gather_kernel, fast), out_shape=(jax.Sha...  31.1 us
    pallas_call x1, Pallas kernels, weight(): pl.pallas_call(weight_kernel, grid=(rows // tile,), in_specs=[smem, smem,...  18.3 us

profile of v1, /device:TPU:0, one launch (start us, length us, event | category | flops | bytes accessed | tf_op | source)
XLA Modules:
  0.0 50.1 jit_solution(13472064889702984946)
XLA Ops:
  0.6 31.1 %gather_and_grad_hidden.1 = (bf16[32,8192]{1,0:T(8,128)(2,1)}, bf16[32,1792]{1,0:T(8,128)(2,1)}, f32[32,64]{1,0:T(8,128)}) custom-call(bf16[2,8192]{1,0:T(2,128)(2,1)} %g_ref.1, bf16[32,1792]{1,0:T(8,128)(2,1)} %hid_ref.3, bf16[64,1792]{1,0:T(8,128)(2,1)} %bitcast.4, bf16[1792,8192]{1,0:T(8,128)(2,1)} %w_ref.1), custom_call_target="tpu_custom_call" | custom-call | tf_op jit(solution)/shard_map/gather_and_grad_hidden/pallas_call | solution.py:144
  31.8 18.3 %grad_weight_and_sketches.1 = (bf16[1792,8192]{1,0:T(8,128)(2,1)}, bf16[32,1792]{1,0:T(8,128)(2,1)}, f32[3,4096]{1,0:T(4,128)}) custom-call(s32[16]{0:T(128)} %len_ref.1, s32[16]{0:T(128)} %cnt_ref.1, s32[1]{0:T(128)} %bitcast.me_ref, bf16[32,1792]{1,0:T(8,128)(2,1)} %hid_ref.3, bf16[32,8192]{1,0:T(8,128)(2,1)} %get-tuple-element.6.all_ref, ...), custom_call_target="tpu_custom_call" | custom-call | tf_op jit(solution)/shard_map/grad_weight_and_sketches/pallas_call | solution.py:222

commit v2 on v1

v2 whole, which is shorter than its diff:
```python
import functools
import jax
import jax.numpy as jnp
from jax import lax
from jax.experimental import pallas as pl
from jax.experimental.pallas import tpu as pltpu
from jax.sharding import PartitionSpec as P

OWN_CAP = 3
SLOW = 4
CUTS = 4
HALVES = 2
NT = (((1,), (1,)), ((), ()))
TN = (((0,), (0,)), ((), ()))
F32 = jnp.float32
BF16 = jnp.bfloat16


def row_tile(width):
    return 256 if width % 256 == 0 else width


def gather_kernel(
    fast, g_ref, hid_ref, pin_ref, w_ref, pout_ref, all_ref, gh_ref, hp_ref, gp_ref,
    buf, wide, wbuf, pbuf, acc, part, stage_a, stage_b, stage_c, wsem, psem,
    s1s, s1r, s2s, s2r, s3s, s3r, pas, par, pbs, pbr, pcs, pcr,
):
    me = lax.axis_index("tensor")
    core = lax.rem(me, 2)
    chip = lax.div(me, 2)
    b = lax.rem(chip, fast)
    a = lax.div(chip, fast)
    cut = buf.shape[-1]
    per = buf.shape[-2]

    def w_copy(c):
        columns = pl.ds(c * cut, cut)
        return pltpu.make_async_copy(w_ref.at[:, columns], wbuf.at[:, columns], wsem.at[c])

    p_copy = pltpu.make_async_copy(pout_ref, pbuf, psem.at[0])
    for c in range(CUTS):
        w_copy(c).start()
        if c == 0:
            p_copy.start()

    def index(ai, bi, ci):
        return (ai * fast + bi) * 2 + ci

    def up(value, step, size):
        return lax.rem(value + step, size)

    def down(value, step, size):
        return lax.rem(value + size - step, size)

    barrier = pltpu.get_barrier_semaphore()
    peers = [index(up(a, s, SLOW), b, core) for s in range(1, SLOW)]
    peers += [index(a, up(b, r, fast), core) for r in range(1, fast)]
    sibling = index(a, b, 1 - core)
    peers += [sibling]
    for peer in peers:
        pl.semaphore_signal(barrier, inc=1, device_id={"tensor": peer}, device_id_type=pl.DeviceIdType.MESH)
    for c in range(CUTS):
        buf[c, core, b, a] = g_ref[:, c * cut : (c + 1) * cut]
    part[0] = lax.dot_general(hid_ref[...], pin_ref[...], NT, preferred_element_type=F32)
    pl.semaphore_wait(barrier, len(peers))

    def send(src, dst, ssem, rsem, peer):
        return pltpu.make_async_remote_copy(
            src_ref=src, dst_ref=dst, send_sem=ssem, recv_sem=rsem,
            device_id={"tensor": peer}, device_id_type=pl.DeviceIdType.MESH,
        )

    sends = []

    def go(src, dst, ssem, rsem, peer):
        copy = send(src, dst, ssem, rsem, peer)
        copy.start()
        sends.append(copy)

    def landed(dst, sem):
        send(dst, dst, sem, sem, sibling).wait_recv()

    def first(c):
        block = buf.at[c, core, b, a]
        for s in (2, 1, 3):
            go(block, block, s1s.at[c, s], s1r.at[c, s], index(up(a, s, SLOW), b, core))

    def second(c):
        for s in range(1, SLOW):
            landed(buf.at[c, core, b, down(a, s, SLOW)], s1r.at[c, s])
        block = buf.at[c, core, b]
        for r in range(1, fast):
            go(block, block, s2s.at[c, r], s2r.at[c, r], index(a, up(b, r, fast), core))

    def third(c):
        for r in range(1, fast):
            landed(buf.at[c, core, down(b, r, fast)], s2r.at[c, r])
        block = buf.at[c, core]
        go(block, block, s3s.at[c], s3r.at[c], sibling)

    def multiply(c):
        landed(buf.at[c, 1 - core], s3r.at[c])
        for ai in range(SLOW):
            for bi in range(fast):
                for ci in range(2):
                    row = index(ai, bi, ci) * per
                    wide[row : row + per, :] = buf[c, ci, bi, ai].astype(F32)
        columns = slice(c * cut, (c + 1) * cut)
        all_ref[:, columns] = wide[...].astype(BF16)
        if c == 0:
            p_copy.wait()
        w_copy(c).wait()
        here = all_ref[:, columns]
        term = lax.dot_general(here, wbuf[:, columns], NT, preferred_element_type=F32)
        own = lax.dot_general(here, pbuf[:, columns], NT, preferred_element_type=F32)
        if c == 0:
            acc[...] = term
            gp_ref[...] = own
        elif c < CUTS - 1:
            acc[...] += term
            gp_ref[...] += own
        else:
            gh_ref[...] = (acc[...] + term).astype(BF16)
            gp_ref[...] += own

    first(0)
    for s in range(1, SLOW):
        go(part.at[0], stage_a.at[s], pas.at[s], par.at[s], index(up(a, s, SLOW), b, core))
    for c in range(1, CUTS):
        first(c)
    second(0)
    second(1)
    third(0)
    total = part[0]
    for s in range(1, SLOW):
        landed(stage_a.at[s], par.at[s])
        total = total + stage_a[s]
    part[1] = total
    for r in range(1, fast):
        go(part.at[1], stage_b.at[r], pbs.at[r], pbr.at[r], index(a, up(b, r, fast), core))
    for c in range(CUTS):
        if c + 2 < CUTS:
            second(c + 2)
        if c + 1 < CUTS:
            third(c + 1)
        if c == 1:
            for r in range(1, fast):
                landed(stage_b.at[r], pbr.at[r])
                total = total + stage_b[r]
            part[2] = total
            go(part.at[2], stage_c.at[0], pcs.at[0], pcr.at[0], sibling)
        multiply(c)

    landed(stage_c.at[0], pcr.at[0])
    hp_ref[...] = part[2] + stage_c[0]
    for copy in sends:
        copy.wait_send()


def gather(tensor, g, hidden, pin_t, w, pout_t):
    per, width = g.shape
    tokens, rows = hidden.shape
    rank = pin_t.shape[0]
    fast = tensor // (2 * SLOW)
    cut = width // CUTS
    dma = pltpu.SemaphoreType.DMA
    vmem = pl.BlockSpec(memory_space=pltpu.VMEM)
    hbm = pl.BlockSpec(memory_space=pl.ANY)
    return pl.pallas_call(
        functools.partial(gather_kernel, fast),
        out_shape=(
            jax.ShapeDtypeStruct((tokens, width), BF16),
            jax.ShapeDtypeStruct((tokens, rows), BF16),
            jax.ShapeDtypeStruct((tokens, rank), F32),
            jax.ShapeDtypeStruct((tokens, rank), F32),
        ),
        in_specs=[vmem, vmem, vmem, hbm, hbm],
        out_specs=(vmem, vmem, vmem, vmem),
        scratch_shapes=[
            pltpu.VMEM((CUTS, 2, fast, SLOW, per, cut), BF16),
            pltpu.VMEM((tokens, cut), F32),
            pltpu.VMEM((rows, width), BF16),
            pltpu.VMEM((rank, width), BF16),
            pltpu.VMEM((tokens, rows), F32),
            pltpu.VMEM((3, tokens, rank), F32),
            pltpu.VMEM((SLOW, tokens, rank), F32),
            pltpu.VMEM((fast, tokens, rank), F32),
            pltpu.VMEM((1, tokens, rank), F32),
            dma((CUTS,)), dma((1,)),
            dma((CUTS, SLOW)), dma((CUTS, SLOW)),
            dma((CUTS, fast)), dma((CUTS, fast)),
            dma((CUTS,)), dma((CUTS,)),
            dma((SLOW,)), dma((SLOW,)),
            dma((fast,)), dma((fast,)),
            dma((1,)), dma((1,)),
        ],
        compiler_params=pltpu.CompilerParams(
            collective_id=0, has_side_effects=True, vmem_limit_bytes=58 * 2**20
        ),
        name="gather_and_grad_hidden",
    )(g, hidden, pin_t, w, pout_t)


def weight_kernel(
    len_ref, cnt_ref, me_ref, hid_ref, all_ref, gh_in, hp_ref, gp_ref,
    gw_ref, gh_ref, sk_ref, obuf, osem,
):
    rows, width = obuf.shape
    tile = row_tile(rows)
    half = width // HALVES
    copies = []
    for i in range(rows // tile):
        for h in range(HALVES):
            at = (pl.ds(i * tile, tile), pl.ds(h * half, half))
            obuf[i * tile : (i + 1) * tile, h * half : (h + 1) * half] = lax.dot_general(
                hid_ref[:, i * tile : (i + 1) * tile], all_ref[:, h * half : (h + 1) * half],
                TN, preferred_element_type=F32,
            ).astype(BF16)
            copy = pltpu.make_async_copy(obuf.at[at], gw_ref.at[at], osem.at[i, h])
            copy.start()
            copies.append(copy)

    gh_ref[...] = gh_in[...]
    tokens, rank = hp_ref.shape
    me = me_ref[0]
    owners = cnt_ref.shape[0]
    examples = len_ref.shape[0]
    first = lax.fori_loop(0, owners, lambda k, c: c + jnp.where(k < me, cnt_ref[k], 0), jnp.int32(0))
    mine = cnt_ref[me]
    gp = jnp.concatenate([gp_ref[...], gp_ref[...]], axis=1)
    t = lax.broadcasted_iota(jnp.int32, (tokens, rank), 0)
    left = lax.broadcasted_iota(jnp.int32, (1, 2 * rank), 1) < rank
    for j in range(OWN_CAP):
        e = first + j
        begin, end = lax.fori_loop(
            0, examples,
            lambda k, c: (c[0] + jnp.where(k < e, len_ref[k], 0), c[1] + jnp.where(k <= e, len_ref[k], 0)),
            (jnp.int32(0), jnp.int32(0)),
        )
        end = jnp.where(j < mine, end, begin)
        hp = jnp.where((t >= begin) & (t < end), hp_ref[...], 0.0)
        s = lax.dot_general(hp, gp, TN, precision=lax.Precision.HIGHEST, preferred_element_type=F32)
        for p in range(rank // 2):
            sk_ref[j : j + 1, 2 * p * rank : 2 * (p + 1) * rank] = jnp.where(
                left, s[2 * p : 2 * p + 1, :], s[2 * p + 1 : 2 * p + 2, :]
            )
    for copy in copies:
        copy.wait()


def weight(hidden, everyone, gh, hp, gp, lengths, counts, me):
    tokens, rows = hidden.shape
    width = everyone.shape[1]
    rank = hp.shape[1]
    smem = pl.BlockSpec(memory_space=pltpu.SMEM)
    vmem = pl.BlockSpec(memory_space=pltpu.VMEM)
    return pl.pallas_call(
        weight_kernel,
        in_specs=[smem] * 3 + [vmem] * 5,
        out_specs=(pl.BlockSpec(memory_space=pl.ANY), vmem, vmem),
        out_shape=(
            jax.ShapeDtypeStruct((rows, width), BF16),
            jax.ShapeDtypeStruct((tokens, rows), BF16),
            jax.ShapeDtypeStruct((OWN_CAP, rank * rank), F32),
        ),
        scratch_shapes=[
            pltpu.VMEM((rows, width), BF16),
            pltpu.SemaphoreType.DMA((rows // row_tile(rows), HALVES)),
        ],
        compiler_params=pltpu.CompilerParams(vmem_limit_bytes=58 * 2**20),
        name="grad_weight_and_sketches",
    )(lengths, counts, me, hidden, everyone, gh, hp, gp)


def solution(mesh):
    tensor = mesh.shape["tensor"]

    def shards(grad_out, hidden, down_weight, proj_in, proj_out, example_lengths, owner_counts):
        everyone, gh, hp, gp = gather(tensor, grad_out, hidden, proj_in.T, down_weight, proj_out.T)
        me = lax.axis_index("tensor").astype(jnp.int32).reshape(1)
        return weight(hidden, everyone, gh, hp, gp, example_lengths, owner_counts, me)

    return jax.shard_map(
        shards,
        mesh=mesh,
        in_specs=(
            P(("groups", "tensor"), None),
            P("groups", "tensor"),
            P("tensor", None),
            P("tensor", None),
            P(),
            P("groups"),
            P("groups"),
        ),
        out_specs=(
            P(("groups", "tensor"), None),
            P("groups", "tensor"),
            P(("groups", "tensor"), None),
        ),
        check_vma=False,
    )
```

time: 50.6 us -> 38.8 us (0.77)
  Pallas kernels: 49.4 us -> 37.8 us
    pallas_call x1, Pallas kernels: 18.3 us -> 12.3 us  [weight(): pl.pallas_call(weight_kernel, in_specs=[smem] * 3 + [vmem] * 5, out_specs...]
    pallas_call x1, Pallas kernels: 31.1 us -> 25.5 us  [gather(): pl.pallas_call(functools.partial(gather_kernel, fast), out_shape=(jax.Sha...]
where the time goes in v2:
time: 38.8 us; the launch traced here: 38.6 us
  Pallas kernels  37.8 us (97%)
  between operations  0.8 us (2%)
    pallas_call x1, Pallas kernels, gather(): pl.pallas_call(functools.partial(gather_kernel, fast), out_shape=(jax.Sha...  25.5 us
    pallas_call x1, Pallas kernels, weight(): pl.pallas_call(weight_kernel, in_specs=[smem] * 3 + [vmem] * 5, out_specs...  12.3 us

profile of v2, /device:TPU:0, one launch (start us, length us, event | category | flops | bytes accessed | tf_op | source)
XLA Modules:
  0.0 38.6 jit_solution(13331767092625341145)
XLA Ops:
  0.6 25.5 %gather_and_grad_hidden.1 = (bf16[32,8192]{1,0:T(8,128)(2,1)}, bf16[32,1792]{1,0:T(8,128)(2,1)}, f32[32,64]{1,0:T(8,128)}, f32[32,64]{1,0:T(8,128)}) custom-call(bf16[2,8192]{1,0:T(2,128)(2,1)} %g_ref.1, bf16[32,1792]{1,0:T(8,128)(2,1)} %hid_ref.3, bf16[64,1792]{1,0:T(8,128)(2,1)} %bitcast.4, bf16[1792,8192]{1,0:T(8,128)(2,1)} %w_ref.1, bf16[64,8192]{1,0:T(8,128)(2,1)} %bitcast.3), custom_call_target="tpu_custom_call" | custom-call | tf_op jit(solution)/shard_map/gather_and_grad_hidden/pallas_call | solution.py:169
  26.2 12.3 %grad_weight_and_sketches.1 = (bf16[1792,8192]{1,0:T(8,128)(2,1)}, bf16[32,1792]{1,0:T(8,128)(2,1)}, f32[3,4096]{1,0:T(4,128)}) custom-call(s32[16]{0:T(128)} %len_ref.1, s32[16]{0:T(128)} %cnt_ref.1, s32[1]{0:T(128)} %bitcast.me_ref, bf16[32,1792]{1,0:T(8,128)(2,1)} %hid_ref.3, bf16[32,8192]{1,0:T(8,128)(2,1)} %get-tuple-element.7.all_ref, ...), custom_call_target="tpu_custom_call" | custom-call | tf_op jit(solution)/shard_map/grad_weight_and_sketches/pallas_call | solution.py:257

commit v3 on v2

--- a/solution.py
+++ b/solution.py
@@ -10,6 +10,8 @@
 SLOW = 4
 CUTS = 4
 HALVES = 2
+FOLD = 16
+LANE = 128
 NT = (((1,), (1,)), ((), ()))
 TN = (((0,), (0,)), ((), ()))
 F32 = jnp.float32
@@ -22,7 +24,7 @@
 
 def gather_kernel(
     fast, g_ref, hid_ref, pin_ref, w_ref, pout_ref, all_ref, gh_ref, hp_ref, gp_ref,
-    buf, wide, wbuf, pbuf, acc, part, stage_a, stage_b, stage_c, wsem, psem,
+    buf, flat, packed, wbuf, pbuf, acc, part, stage_a, stage_b, stage_c, wsem, psem,
     s1s, s1r, s2s, s2r, s3s, s3r, pas, par, pbs, pbr, pcs, pcr,
 ):
     me = lax.axis_index("tensor")
@@ -30,8 +32,12 @@
     chip = lax.div(me, 2)
     b = lax.rem(chip, fast)
     a = lax.div(chip, fast)
-    cut = buf.shape[-1]
-    per = buf.shape[-2]
+    per = g_ref.shape[0]
+    cut = g_ref.shape[1] // CUTS
+    tokens = hid_ref.shape[0]
+    folds = FOLD // per
+    lanes = cut // (folds * LANE)
+    columns_of = cut // LANE
 
     def w_copy(c):
         columns = pl.ds(c * cut, cut)
@@ -60,7 +66,13 @@
     for peer in peers:
         pl.semaphore_signal(barrier, inc=1, device_id={"tensor": peer}, device_id_type=pl.DeviceIdType.MESH)
     for c in range(CUTS):
-        buf[c, core, b, a] = g_ref[:, c * cut : (c + 1) * cut]
+        mine = g_ref[:, c * cut : (c + 1) * cut].astype(F32)
+        for t in range(per):
+            for j in range(folds):
+                packed[t * folds + j : t * folds + j + 1, :] = mine[
+                    t : t + 1, j * lanes * LANE : (j + 1) * lanes * LANE
+                ]
+        buf[c, core, b, a] = packed[...].astype(BF16)
     part[0] = lax.dot_general(hid_ref[...], pin_ref[...], NT, preferred_element_type=F32)
     pl.semaphore_wait(barrier, len(peers))
 
@@ -103,10 +115,21 @@
         for ai in range(SLOW):
             for bi in range(fast):
                 for ci in range(2):
-                    row = index(ai, bi, ci) * per
-                    wide[row : row + per, :] = buf[c, ci, bi, ai].astype(F32)
+                    block = buf[c, ci, bi, ai].astype(F32)
+                    for t in range(per):
+                        group, row = divmod(index(ai, bi, ci) * per + t, 8)
+                        for l in range(lanes):
+                            flat[pl.ds((group * columns_of + l) * 8 + row, folds, stride=lanes * 8), :] = block[
+                                t * folds : (t + 1) * folds, l * LANE : (l + 1) * LANE
+                            ]
+        for k in range(columns_of):
+            for q in range(tokens // 16):
+                top = (2 * q * columns_of + k) * 8
+                low = ((2 * q + 1) * columns_of + k) * 8
+                all_ref[q * 16 : (q + 1) * 16, c * cut + k * LANE : c * cut + (k + 1) * LANE] = jnp.concatenate(
+                    [flat[top : top + 8, :], flat[low : low + 8, :]], axis=0
+                ).astype(BF16)
         columns = slice(c * cut, (c + 1) * cut)
-        all_ref[:, columns] = wide[...].astype(BF16)
         if c == 0:
             p_copy.wait()
         w_copy(c).wait()
@@ -177,8 +200,9 @@
         in_specs=[vmem, vmem, vmem, hbm, hbm],
         out_specs=(vmem, vmem, vmem, vmem),
         scratch_shapes=[
-            pltpu.VMEM((CUTS, 2, fast, SLOW, per, cut), BF16),
-            pltpu.VMEM((tokens, cut), F32),
+            pltpu.VMEM((CUTS, 2, fast, SLOW, FOLD, per * cut // FOLD), BF16),
+            pltpu.VMEM((tokens * cut // LANE, LANE), F32),
+            pltpu.VMEM((FOLD, per * cut // FOLD), F32),
             pltpu.VMEM((rows, width), BF16),
             pltpu.VMEM((rank, width), BF16),
             pltpu.VMEM((tokens, rows), F32),

time: 38.8 us -> 38.8 us (level)
  no operation moved by 1% of the time
where the time goes in v3:
time: 38.8 us; the launch traced here: 38.7 us
  Pallas kernels  37.9 us (98%)
  between operations  0.8 us (2%)
    pallas_call x1, Pallas kernels, gather(): pl.pallas_call(functools.partial(gather_kernel, fast), out_shape=(jax.Sha...  25.6 us
    pallas_call x1, Pallas kernels, weight(): pl.pallas_call(weight_kernel, in_specs=[smem] * 3 + [vmem] * 5, out_specs...  12.3 us

profile of v3, /device:TPU:0, one launch (start us, length us, event | category | flops | bytes accessed | tf_op | source)
XLA Modules:
  0.0 38.7 jit_solution(4461790416266627838)
XLA Ops:
  0.6 25.6 %gather_and_grad_hidden.1 = (bf16[32,8192]{1,0:T(8,128)(2,1)}, bf16[32,1792]{1,0:T(8,128)(2,1)}, f32[32,64]{1,0:T(8,128)}, f32[32,64]{1,0:T(8,128)}) custom-call(bf16[2,8192]{1,0:T(2,128)(2,1)} %g_ref.1, bf16[32,1792]{1,0:T(8,128)(2,1)} %hid_ref.3, bf16[64,1792]{1,0:T(8,128)(2,1)} %bitcast.4, bf16[1792,8192]{1,0:T(8,128)(2,1)} %w_ref.1, bf16[64,8192]{1,0:T(8,128)(2,1)} %bitcast.3), custom_call_target="tpu_custom_call" | custom-call | tf_op jit(solution)/shard_map/gather_and_grad_hidden/pallas_call | solution.py:192
  26.2 12.3 %grad_weight_and_sketches.1 = (bf16[1792,8192]{1,0:T(8,128)(2,1)}, bf16[32,1792]{1,0:T(8,128)(2,1)}, f32[3,4096]{1,0:T(4,128)}) custom-call(s32[16]{0:T(128)} %len_ref.1, s32[16]{0:T(128)} %cnt_ref.1, s32[1]{0:T(128)} %bitcast.me_ref, bf16[32,1792]{1,0:T(8,128)(2,1)} %hid_ref.3, bf16[32,8192]{1,0:T(8,128)(2,1)} %get-tuple-element.7.all_ref, ...), custom_call_target="tpu_custom_call" | custom-call | tf_op jit(solution)/shard_map/grad_weight_and_sketches/pallas_call | solution.py:281

commit v4 on v2

--- a/solution.py
+++ b/solution.py
@@ -91,15 +91,17 @@
         block = buf.at[c, core, b]
         for r in range(1, fast):
             go(block, block, s2s.at[c, r], s2r.at[c, r], index(a, up(b, r, fast), core))
+        go(block, block, s3s.at[c, 0], s3r.at[c, 0], sibling)
 
     def third(c):
         for r in range(1, fast):
-            landed(buf.at[c, core, down(b, r, fast)], s2r.at[c, r])
-        block = buf.at[c, core]
-        go(block, block, s3s.at[c], s3r.at[c], sibling)
+            block = buf.at[c, core, down(b, r, fast)]
+            landed(block, s2r.at[c, r])
+            go(block, block, s3s.at[c, r], s3r.at[c, r], sibling)
 
     def multiply(c):
-        landed(buf.at[c, 1 - core], s3r.at[c])
+        for r in range(fast):
+            landed(buf.at[c, 1 - core, down(b, r, fast)], s3r.at[c, r])
         for ai in range(SLOW):
             for bi in range(fast):
                 for ci in range(2):
@@ -189,7 +191,7 @@
             dma((CUTS,)), dma((1,)),
             dma((CUTS, SLOW)), dma((CUTS, SLOW)),
             dma((CUTS, fast)), dma((CUTS, fast)),
-            dma((CUTS,)), dma((CUTS,)),
+            dma((CUTS, fast)), dma((CUTS, fast)),
             dma((SLOW,)), dma((SLOW,)),
             dma((fast,)), dma((fast,)),
             dma((1,)), dma((1,)),

time: 38.8 us -> 38.9 us (level)
  no operation moved by 1% of the time
where the time goes in v4:
time: 38.9 us; the launch traced here: 38.7 us
  Pallas kernels  37.9 us (97%)
  between operations  0.8 us (2%)
    pallas_call x1, Pallas kernels, gather(): pl.pallas_call(functools.partial(gather_kernel, fast), out_shape=(jax.Sha...  25.6 us
    pallas_call x1, Pallas kernels, weight(): pl.pallas_call(weight_kernel, in_specs=[smem] * 3 + [vmem] * 5, out_specs...  12.3 us

profile of v4, /device:TPU:0, one launch (start us, length us, event | category | flops | bytes accessed | tf_op | source)
XLA Modules:
  0.0 38.7 jit_solution(14591420639595880002)
XLA Ops:
  0.6 25.6 %gather_and_grad_hidden.1 = (bf16[32,8192]{1,0:T(8,128)(2,1)}, bf16[32,1792]{1,0:T(8,128)(2,1)}, f32[32,64]{1,0:T(8,128)}, f32[32,64]{1,0:T(8,128)}) custom-call(bf16[2,8192]{1,0:T(2,128)(2,1)} %g_ref.1, bf16[32,1792]{1,0:T(8,128)(2,1)} %hid_ref.3, bf16[64,1792]{1,0:T(8,128)(2,1)} %bitcast.4, bf16[1792,8192]{1,0:T(8,128)(2,1)} %w_ref.1, bf16[64,8192]{1,0:T(8,128)(2,1)} %bitcast.3), custom_call_target="tpu_custom_call" | custom-call | tf_op jit(solution)/shard_map/gather_and_grad_hidden/pallas_call | solution.py:171
  26.3 12.3 %grad_weight_and_sketches.1 = (bf16[1792,8192]{1,0:T(8,128)(2,1)}, bf16[32,1792]{1,0:T(8,128)(2,1)}, f32[3,4096]{1,0:T(4,128)}) custom-call(s32[16]{0:T(128)} %len_ref.1, s32[16]{0:T(128)} %cnt_ref.1, s32[1]{0:T(128)} %bitcast.me_ref, bf16[32,1792]{1,0:T(8,128)(2,1)} %hid_ref.3, bf16[32,8192]{1,0:T(8,128)(2,1)} %get-tuple-element.7.all_ref, ...), custom_call_target="tpu_custom_call" | custom-call | tf_op jit(solution)/shard_map/grad_weight_and_sketches/pallas_call | solution.py:259
